TPU v7x, 32 devices: a whole 2x2x4 slice. The times are simulated.
32 devices in a mesh: tm: 32 (over z, y, x, core).
Axes of the slice: x: 2, y: 2, z: 4, core: 2. Of those that a mesh axis runs over, the one named last changes fastest.
Arguments:
- observations: float32 [1024, 4, 64], P('tm'), may hold values from -6 to 6
- decay: float32 [1024, 128], P('tm'), may hold values from 0 to 1
- transition: float32 [128, 128], replicated, may hold values from -1 to 1
- obs_map: float32 [64, 128], replicated, may hold values from -0.0625 to 0.0625
- noise_precision: float32 [64], replicated, may hold values from 0.01 to 0.2
- smoother_gain: float32 [128, 128], replicated, may hold values from -1 to 1
Outputs:
- filtered: float32 [1024, 4, 128], P('tm')
- smoothed: float32 [1024, 4, 128], P('tm')
All inputs are finite; a program needn't handle non-finite values.
Results may differ from a plain program's by a relative error of at most 0.0003.
Values sent between devices are 32-bit elements; how exact they have to be, the bound alone decides.
A program may use at most 128 MiB of HBM per device.

v0:
```python
import functools

import jax
import jax.numpy as jnp
from jax import lax
from jax.experimental import pallas as pl
from jax.experimental.pallas import tpu as pltpu
from jax.sharding import PartitionSpec as P

MESH = pl.DeviceIdType.MESH
F32, BF16 = jnp.float32, jnp.bfloat16
S = 128
Q = 4
SUBS = 4


def halves(x):
    high = x.astype(BF16)
    low = (x - high.astype(F32)).astype(BF16)
    return jnp.concatenate([high, low], axis=1)


def weights(m):
    both = halves(m)
    return jnp.concatenate([both, both], axis=0)


def mul(x, w):
    y = jnp.dot(halves(x), w, preferred_element_type=F32)
    return y[:, :S] + y[:, S:]


def spread(row, rows):
    return jnp.broadcast_to(row, (rows, S))


def padded(x):
    return jnp.concatenate([x, jnp.zeros((8 - x.shape[0], S), F32)], axis=0)


def parts(m):
    return m[:S], m[S : S + 8], m[S + 8 :]


def compose(earlier, later):
    later_map, later_add, later_decay = parts(later)
    y = mul(earlier[: S + 8] * later_decay[:1], weights(later_map))
    return jnp.concatenate([y[:S], y[S:] + later_add, earlier[S + 8 :]], axis=0)


def pick(index, options):
    chosen = options[0]
    for k in range(1, len(options)):
        chosen = jnp.where(index == k, options[k], chosen)
    return chosen


def kernel(
    n,
    levels,
    obs_ref,
    dec_ref,
    trans_ref,
    map_ref,
    noise_ref,
    gain_ref,
    filt_ref,
    smooth_ref,
    u_ref,
    dx_ref,
    g_ref,
    next_ref,
    next_send,
    next_recv,
    *rest,
):
    count = len(levels)
    f_bufs, z_bufs, y_bufs = rest[:count], rest[count : 2 * count], rest[2 * count : 3 * count]
    send_sem, recv_sem = rest[3 * count :]
    me = lax.axis_index("tm")
    steps = dec_ref.shape[0]
    length = steps // SUBS
    digits = [(me // stride) % radix for radix, stride in levels]

    barrier = pltpu.get_barrier_semaphore()
    greeted = 0
    for (radix, stride), digit in zip(levels, digits):
        for ahead in range(1, radix):
            other = me + ((digit + ahead) % radix - digit) * stride
            pl.semaphore_signal(barrier, inc=1, device_id=(other,), device_id_type=MESH)
            greeted += 1
    pl.semaphore_signal(barrier, inc=1, device_id=((me + 1) % n,), device_id_type=MESH)
    greeted += 1

    def send(which, level, bufs, own):
        radix, stride = levels[level]
        digit = digits[level]
        bufs[level][digit] = own
        copies = []
        for ahead in range(1, radix):
            other = me + ((digit + ahead) % radix - digit) * stride
            copy = pltpu.make_async_remote_copy(
                src_ref=bufs[level].at[digit],
                dst_ref=bufs[level].at[digit],
                send_sem=send_sem.at[which, level, ahead - 1],
                recv_sem=recv_sem.at[which, level, ahead - 1],
                device_id=(other,),
                device_id_type=MESH,
            )
            copy.start()
            copies.append(copy)
        sent.extend(copies)
        return copies

    sent = []
    highest = lax.Precision.HIGHEST
    trans_t, gain_t = trans_ref[...].T, gain_ref[...].T
    obs_map, noise = map_ref[...], noise_ref[...]
    closed = trans_t - jnp.dot(
        trans_t,
        jnp.dot(obs_map.T * noise, obs_map, precision=highest, preferred_element_type=F32),
        precision=highest,
        preferred_element_type=F32,
    )
    w_closed, w_gain, w_trans = weights(closed), weights(gain_t), weights(trans_t)
    u_ref[...] = jnp.dot(
        obs_ref[...] * noise, obs_map, precision=highest, preferred_element_type=F32
    )
    dec = [dec_ref[t : t + 1, :] for t in range(steps)]
    for t in range(steps):
        dx_ref[t * Q : (t + 1) * Q, :] = spread(dec[t], Q)

    def at(ref, i):
        return jnp.concatenate(
            [ref[(b * length + i) * Q : (b * length + i + 1) * Q, :] for b in range(SUBS)], axis=0
        )

    def decayed(x, i):
        return [x[b * S : (b + 1) * S] * dec[b * length + i] for b in range(SUBS)]

    maps = jnp.concatenate([closed] * SUBS, axis=0)
    adds = at(u_ref, 0)
    back = jnp.concatenate([gain_t] * SUBS, axis=0)
    for i in range(1, length):
        y = mul(jnp.concatenate(decayed(maps, i) + [adds * at(dx_ref, i)], axis=0), w_closed)
        maps, adds = y[: SUBS * S], y[SUBS * S :] + at(u_ref, i)
        back = mul(jnp.concatenate(decayed(back, length - i), axis=0), w_gain)
    sub = [
        jnp.concatenate(
            [
                maps[b * S : (b + 1) * S],
                padded(adds[b * Q : (b + 1) * Q]),
                spread(dec[b * length], 8),
            ],
            axis=0,
        )
        for b in range(SUBS)
    ]
    sub_back = decayed(back, 0)
    total = compose(compose(sub[0], sub[1]), compose(sub[2], sub[3]))

    pl.semaphore_wait(barrier, greeted)
    waiting = send(0, 0, f_bufs, total)
    next_copy = pltpu.make_async_remote_copy(
        src_ref=dec_ref.at[pl.ds(0, 8)],
        dst_ref=next_ref,
        send_sem=next_send,
        recv_sem=next_recv,
        device_id=((me + n - 1) % n,),
        device_id_type=MESH,
    )
    next_copy.start()
    z_total = mul(
        mul(sub_back[3], weights(sub_back[2])), weights(mul(sub_back[1], weights(sub_back[0])))
    )
    z_waiting = send(1, 0, z_bufs, z_total)

    eye = jnp.where(
        lax.broadcasted_iota(jnp.int32, (S, S), 0) == lax.broadcasted_iota(jnp.int32, (S, S), 1),
        1.0,
        0.0,
    ).astype(F32)
    identity = jnp.concatenate([eye, jnp.zeros((8, S), F32), jnp.ones((8, S), F32)], axis=0)

    prefix = None
    suffixes = [None]
    w_later = []
    for level, (radix, stride) in enumerate(levels):
        digit = digits[level]
        last = level == count - 1
        if level > 0:
            below, lower = levels[level - 1][0], digits[level - 1]
            for copy in z_waiting:
                copy.wait_recv()
            z = [z_bufs[level - 1][k] for k in range(below)]
            w_z = [weights(z[k]) for k in range(below - 1)]
            w_later.append(w_z)
            run = z[below - 1]
            options = [eye]
            for k in range(below - 2, -1, -1):
                options.insert(0, run)
                run = mul(run, w_z[k])
            z_waiting = send(1, level, z_bufs, run)
            suffix = pick(lower, options)
            if suffixes[-1] is not None:
                suffix = mul(suffix, weights(suffixes[-1]))
            suffixes.append(suffix)
        for copy in waiting:
            copy.wait_recv()
        m = [f_bufs[level][k] for k in range(radix)]
        if not last:
            if radix == 2:
                options = [identity, m[0]]
                total = compose(m[0], m[1])
            else:
                first = compose(m[0], m[1])
                total = compose(first, compose(m[2], m[3]))
                options = [identity, m[0], first, compose(first, m[2])]
            waiting = send(0, level + 1, f_bufs, total)
            here = pick(digit, options)
            prefix = here if prefix is None else compose(here, prefix)
        else:
            state = parts(m[0])[1]
            options = [jnp.zeros((8, S), F32), state]
            for k in range(1, radix - 1):
                one_map, one_add, one_decay = parts(m[k])
                state = mul(state * one_decay, weights(one_map)) + one_add
                options.append(state)
            own_map, own_add, own_decay = parts(prefix)
            entering = mul(pick(digit, options) * own_decay, weights(own_map)) + own_add

    starts = [entering]
    for b in range(SUBS - 1):
        one_map, one_add, one_decay = parts(sub[b])
        starts.append(mul(starts[-1] * one_decay, weights(one_map)) + one_add)
    x = jnp.concatenate([s[:Q] for s in starts], axis=0)
    for i in range(length):
        x = mul(x * at(dx_ref, i), w_closed) + at(u_ref, i)
        for b in range(SUBS):
            filt_ref[(b * length + i) * Q : (b * length + i + 1) * Q, :] = x[b * Q : (b + 1) * Q]

    next_copy.wait_recv()
    following = jnp.where(me == n - 1, 0.0, next_ref[:1, :])
    dx_ref[steps * Q : (steps + 1) * Q, :] = spread(following, Q)
    ahead_decay = dx_ref[Q : (steps + 1) * Q, :]
    filtered = filt_ref[...]
    predicted = mul(filtered * ahead_decay, w_trans)
    g_ref[...] = filtered - mul(predicted * ahead_decay, w_gain)

    s = at(g_ref, length - 1)
    for i in range(length - 2, -1, -1):
        s = mul(s * at(dx_ref, i + 1), w_gain) + at(g_ref, i)
    s = s * at(dx_ref, 0)
    r = [padded(s[b * Q : (b + 1) * Q]) for b in range(SUBS)]
    w_sub = [weights(sub_back[b]) for b in range(SUBS)]
    y = r[SUBS - 1]
    for b in range(SUBS - 2, -1, -1):
        y = mul(y, w_sub[b]) + r[b]

    arriving = None
    for level, (radix, stride) in enumerate(levels):
        last = level == count - 1
        y_waiting = send(2, level, y_bufs, y)
        if last:
            for copy in z_waiting:
                copy.wait_recv()
            w_later.append([weights(z_bufs[level][k]) for k in range(radix - 1)])
        for copy in y_waiting:
            copy.wait_recv()
        run = y_bufs[level][radix - 1]
        options = [jnp.zeros((8, S), F32)]
        for k in range(radix - 2, -1, -1):
            options.insert(0, run)
            if k > 0 or not last:
                run = mul(run, w_later[level][k]) + y_bufs[level][k]
        y = run
        here = pick(digits[level], options)
        if arriving is None:
            arriving = here
        else:
            arriving = arriving + mul(here, weights(suffixes[level]))

    ends = [arriving]
    for b in range(SUBS - 1, 0, -1):
        ends.insert(0, mul(ends[0], w_sub[b]) + r[b])
    x = jnp.concatenate([e[:Q] for e in ends], axis=0)
    for i in range(length - 1, -1, -1):
        s = mul(x, w_gain) + at(g_ref, i)
        for b in range(SUBS):
            smooth_ref[(b * length + i) * Q : (b * length + i + 1) * Q, :] = s[b * Q : (b + 1) * Q]
        x = s * at(dx_ref, i)

    for copy in sent:
        copy.wait_send()
    next_copy.wait_send()


def levels_of(n):
    levels, stride = [], 1
    while stride < n:
        radix = 4 if stride > 1 and n // stride % 4 == 0 else 2
        levels.append((radix, stride))
        stride *= radix
    return levels


def solution(mesh):
    n = mesh.shape["tm"]
    levels = levels_of(n)

    def local(observations, decay, transition, obs_map, noise_precision, smoother_gain):
        steps, records, channels = observations.shape
        rows = steps * records
        out = jax.ShapeDtypeStruct((rows, S), F32)
        vmem = pl.BlockSpec(memory_space=pltpu.VMEM)
        filtered, smoothed = pl.pallas_call(
            functools.partial(kernel, n, levels),
            out_shape=(out, out),
            in_specs=[vmem] * 6,
            out_specs=(vmem, vmem),
            scratch_shapes=[
                pltpu.VMEM((rows, S), F32),
                pltpu.VMEM((rows + 8, S), F32),
                pltpu.VMEM((rows, S), F32),
                pltpu.VMEM((8, S), F32),
                pltpu.SemaphoreType.DMA,
                pltpu.SemaphoreType.DMA,
            ]
            + [pltpu.VMEM((radix, S + 16, S), F32) for radix, _ in levels]
            + [pltpu.VMEM((radix, S, S), F32) for radix, _ in levels]
            + [pltpu.VMEM((radix, 8, S), F32) for radix, _ in levels]
            + [pltpu.SemaphoreType.DMA((3, len(levels), 3))] * 2,
            compiler_params=pltpu.CompilerParams(
                collective_id=0, has_side_effects=True, vmem_limit_bytes=48 * 2**20
            ),
        )(
            observations.reshape(rows, channels),
            decay,
            transition,
            obs_map,
            noise_precision.reshape(1, channels),
            smoother_gain,
        )
        return filtered.reshape(steps, records, S), smoothed.reshape(steps, records, S)

    in_specs = (P("tm", None, None), P("tm", None), P(), P(), P(), P())
    out_specs = (P("tm", None, None), P("tm", None, None))
    return jax.shard_map(local, mesh=mesh, in_specs=in_specs, out_specs=out_specs, check_vma=False)
```

profile of v0, /device:TPU:0, one launch (start us, length us, event | category | flops | bytes accessed | tf_op | source)
XLA Modules:
  0.0 42.3 jit_solution(834527533721254055)
XLA Ops:
  0.6 0.0 copy-start.5
  0.6 0.6 %copy-done.5 = f32[64]{0:T(128)S(1)} copy-done((f32[64]{0:T(128)S(1)}, f32[64]{0:T(128)}, u32[]{:S(2)}) %copy-start.5) | copy-done | bytes 280
  1.3 0.0 copy-start
  1.3 0.8 %copy-done = f32[32,4,64]{2,1,0:T(4,128)S(1)} copy-done((f32[32,4,64]{2,1,0:T(4,128)S(1)}, f32[32,4,64]{2,1,0:T(4,128)}, u32[]{:S(2)}) %copy-start) | copy-done | bytes 32792
  2.1 0.0 copy-start.1
  2.1 0.8 %copy-done.1 = f32[128,128]{1,0:T(8,128)S(1)} copy-done((f32[128,128]{1,0:T(8,128)S(1)}, f32[128,128]{1,0:T(8,128)}, u32[]{:S(2)}) %copy-start.1) | copy-done | bytes 65560
  3.0 0.0 copy-start.2
  3.0 0.8 %copy-done.2 = f32[128,128]{1,0:T(8,128)S(1)} copy-done((f32[128,128]{1,0:T(8,128)S(1)}, f32[128,128]{1,0:T(8,128)}, u32[]{:S(2)}) %copy-start.2) | copy-done | bytes 65560
  3.8 0.0 copy-start.3
  3.8 0.8 %copy-done.3 = f32[64,128]{1,0:T(8,128)S(1)} copy-done((f32[64,128]{1,0:T(8,128)S(1)}, f32[64,128]{1,0:T(8,128)}, u32[]{:S(2)}) %copy-start.3) | copy-done | bytes 32792
  4.6 0.0 copy-start.4
  4.6 0.7 %copy-done.4 = f32[32,128]{1,0:T(8,128)S(1)} copy-done((f32[32,128]{1,0:T(8,128)S(1)}, f32[32,128]{1,0:T(8,128)}, u32[]{:S(2)}) %copy-start.4) | copy-done | bytes 16408
  5.3 35.7 %shard_map.77 = (f32[128,128]{1,0:T(8,128)S(1)}, f32[128,128]{1,0:T(8,128)S(1)}) custom-call(f32[128,64]{1,0:T(8,128)S(1)} %bitcast.6, f32[32,128]{1,0:T(8,128)S(1)} %copy-done.4, f32[128,128]{1,0:T(8,128)S(1)} %copy-done.1, f32[64,128]{1,0:T(8,128)S(1)} %copy-done.3, f32[1,64]{1,0:T(1,128)S(1)} %bitcast.7, f32[128,128]{1,0:T(8,128)S(1)} %copy-done.2), custom_call_target="tpu_custom_call" | custom-call | tf_op jit(solution)/shard_map/pallas_call | solution.py:316
  41.0 0.6 %copy.10 = f32[32,4,128]{2,1,0:T(4,128)} copy(f32[32,4,128]{2,1,0:T(4,128)S(1)} %bitcast.5) | data formatting | bytes 131072
  41.7 0.6 %copy.11 = f32[32,4,128]{2,1,0:T(4,128)} copy(f32[32,4,128]{2,1,0:T(4,128)S(1)} %bitcast.4) | data formatting | bytes 131072
Async XLA Ops:
  0.6 0.7 %copy-start.5 = (f32[64]{0:T(128)S(1)}, f32[64]{0:T(128)}, u32[]{:S(2)}) copy-start(f32[64]{0:T(128)} %param.10) | copy-start | bytes 772
  1.3 0.8 %copy-start = (f32[32,4,64]{2,1,0:T(4,128)S(1)}, f32[32,4,64]{2,1,0:T(4,128)}, u32[]{:S(2)}) copy-start(f32[32,4,64]{2,1,0:T(4,128)} %param.6) | copy-start | bytes 98308
  2.1 0.8 %copy-start.1 = (f32[128,128]{1,0:T(8,128)S(1)}, f32[128,128]{1,0:T(8,128)}, u32[]{:S(2)}) copy-start(f32[128,128]{1,0:T(8,128)} %trans_ref.1) | copy-start | bytes 196612
  3.0 0.8 %copy-start.2 = (f32[128,128]{1,0:T(8,128)S(1)}, f32[128,128]{1,0:T(8,128)}, u32[]{:S(2)}) copy-start(f32[128,128]{1,0:T(8,128)} %gain_ref.1) | copy-start | bytes 196612
  3.8 0.8 %copy-start.3 = (f32[64,128]{1,0:T(8,128)S(1)}, f32[64,128]{1,0:T(8,128)}, u32[]{:S(2)}) copy-start(f32[64,128]{1,0:T(8,128)} %map_ref.1) | copy-start | bytes 98308
  4.6 0.7 %copy-start.4 = (f32[32,128]{1,0:T(8,128)S(1)}, f32[32,128]{1,0:T(8,128)}, u32[]{:S(2)}) copy-start(f32[32,128]{1,0:T(8,128)} %dec_ref.1) | copy-start | bytes 49156
where the time goes:
time: 42.7 us; the launch traced here: 42.3 us
  Pallas kernels  35.7 us (84%)
  local copies, waits for them, and re-layouts  5.9 us (14%)
  between operations  0.65 us (2%)
    pallas_call x1, Pallas kernels, local(): pl.pallas_call(functools.partial(kernel, n, levels), out_shape=(out, out)...  35.7 us
    unnamed x14, local copies, waits for them, and re-layouts  5.9 us

commit v1 on v0

--- a/solution.py
+++ b/solution.py
@@ -58,6 +58,14 @@
 def kernel(
     n,
     levels,
+    obs_in,
+    dec_in,
+    trans_in,
+    map_in,
+    noise_in,
+    gain_in,
+    filt_out,
+    smooth_out,
     obs_ref,
     dec_ref,
     trans_ref,
@@ -66,6 +74,8 @@
     gain_ref,
     filt_ref,
     smooth_ref,
+    in_sem,
+    out_sem,
     u_ref,
     dx_ref,
     g_ref,
@@ -75,8 +85,24 @@
     *rest,
 ):
     count = len(levels)
-    f_bufs, z_bufs, y_bufs = rest[:count], rest[count : 2 * count], rest[2 * count : 3 * count]
-    send_sem, recv_sem = rest[3 * count :]
+    f_bufs, rest = rest[: count - 1], rest[count - 1 :]
+    z_bufs, y_bufs, rest = rest[:count], rest[count : 2 * count], rest[2 * count :]
+    own_ref, third_ref, back_ref, edge_ref, send_sem, recv_sem, edge_send, edge_recv = rest
+    fetched = [
+        pltpu.make_async_copy(a, b, in_sem.at[k])
+        for k, (a, b) in enumerate(
+            [
+                (trans_in, trans_ref),
+                (map_in, map_ref),
+                (noise_in, noise_ref),
+                (gain_in, gain_ref),
+                (dec_in, dec_ref),
+                (obs_in, obs_ref),
+            ]
+        )
+    ]
+    for copy in fetched:
+        copy.start()
     me = lax.axis_index("tm")
     steps = dec_ref.shape[0]
     length = steps // SUBS
@@ -113,6 +139,8 @@
         return copies
 
     sent = []
+    for copy in fetched:
+        copy.wait()
     highest = lax.Precision.HIGHEST
     trans_t, gain_t = trans_ref[...].T, gain_ref[...].T
     obs_map, noise = map_ref[...], noise_ref[...]
@@ -182,52 +210,102 @@
     ).astype(F32)
     identity = jnp.concatenate([eye, jnp.zeros((8, S), F32), jnp.ones((8, S), F32)], axis=0)
 
+    def take_back(level, waiting, suffix):
+        radix = levels[level][0]
+        for copy in waiting:
+            copy.wait_recv()
+        z = [z_bufs[level][k] for k in range(radix)]
+        w_z = [weights(z[k]) for k in range(radix - 1)]
+        w_later.append(w_z)
+        run = z[radix - 1]
+        options = [eye]
+        for k in range(radix - 2, -1, -1):
+            options.insert(0, run)
+            run = mul(run, w_z[k])
+        here = pick(digits[level], options)
+        return run, here if suffix is None else mul(here, weights(suffix))
+
+    def along(source, target, send_at, recv_at, by):
+        return pltpu.make_async_remote_copy(
+            src_ref=source,
+            dst_ref=target,
+            send_sem=edge_send.at[send_at],
+            recv_sem=edge_recv.at[recv_at],
+            device_id=(me + by * levels[-1][1],),
+            device_id_type=MESH,
+        )
+
+    top = digits[-1]
+    first_add = along(own_ref.at[pl.ds(S, 8)], edge_ref.at[0], 0, 0, 1)
+    both_add = [along(edge_ref.at[2], edge_ref.at[1], k, 1, k) for k in (1, 2)]
+    third = along(own_ref, third_ref, 0, 2, 1)
+    back_two = [along(back_ref, z_bufs[-1].at[2], k, 4, -k) for k in (1, 2)]
+    back_one = along(back_ref, z_bufs[-1].at[1], 1, 3, -1)
+
+    w_later, suffixes = [], [None]
     prefix = None
-    suffixes = [None]
-    w_later = []
-    for level, (radix, stride) in enumerate(levels):
-        digit = digits[level]
-        last = level == count - 1
-        if level > 0:
-            below, lower = levels[level - 1][0], digits[level - 1]
-            for copy in z_waiting:
-                copy.wait_recv()
-            z = [z_bufs[level - 1][k] for k in range(below)]
-            w_z = [weights(z[k]) for k in range(below - 1)]
-            w_later.append(w_z)
-            run = z[below - 1]
-            options = [eye]
-            for k in range(below - 2, -1, -1):
-                options.insert(0, run)
-                run = mul(run, w_z[k])
-            z_waiting = send(1, level, z_bufs, run)
-            suffix = pick(lower, options)
-            if suffixes[-1] is not None:
-                suffix = mul(suffix, weights(suffixes[-1]))
-            suffixes.append(suffix)
+    for level in range(count - 1):
+        radix = levels[level][0]
         for copy in waiting:
             copy.wait_recv()
         m = [f_bufs[level][k] for k in range(radix)]
-        if not last:
-            if radix == 2:
-                options = [identity, m[0]]
-                total = compose(m[0], m[1])
-            else:
-                first = compose(m[0], m[1])
-                total = compose(first, compose(m[2], m[3]))
-                options = [identity, m[0], first, compose(first, m[2])]
+        if radix == 2:
+            options = [identity, m[0]]
+            total = compose(m[0], m[1])
+        else:
+            first = compose(m[0], m[1])
+            total = compose(first, compose(m[2], m[3]))
+        if level < count - 2:
             waiting = send(0, level + 1, f_bufs, total)
-            here = pick(digit, options)
-            prefix = here if prefix is None else compose(here, prefix)
         else:
-            state = parts(m[0])[1]
-            options = [jnp.zeros((8, S), F32), state]
-            for k in range(1, radix - 1):
-                one_map, one_add, one_decay = parts(m[k])
-                state = mul(state * one_decay, weights(one_map)) + one_add
-                options.append(state)
-            own_map, own_add, own_decay = parts(prefix)
-            entering = mul(pick(digit, options) * own_decay, weights(own_map)) + own_add
+            own_ref[...] = total
+
+            @pl.when(top == 0)
+            def _():
+                first_add.start()
+
+            @pl.when(top == 2)
+            def _():
+                third.start()
+
+        if level > 0:
+            z_waiting = send(1, level, z_bufs, z_total)
+        if radix == 4:
+            options = [identity, m[0], first, compose(first, m[2])]
+        here = pick(digits[level], options)
+        prefix = here if prefix is None else compose(here, prefix)
+        if level < count - 2:
+            z_total, suffix = take_back(level, z_waiting, suffixes[-1])
+            suffixes.append(suffix)
+
+    edge_ref[3] = jnp.zeros((8, S), F32)
+    own_map, own_add, own_decay = parts(total)
+    w_own = weights(own_map)
+
+    @pl.when(top == 1)
+    def _():
+        first_add.wait_recv()
+        state = edge_ref[0]
+        edge_ref[3] = state
+        edge_ref[2] = mul(state * own_decay, w_own) + own_add
+        for copy in both_add:
+            copy.start()
+
+    @pl.when(top == 2)
+    def _():
+        both_add[0].wait_recv()
+        edge_ref[3] = edge_ref[1]
+
+    @pl.when(top == 3)
+    def _():
+        third.wait_recv()
+        one_map, one_add, one_decay = parts(third_ref[...])
+        w_one = weights(one_map)
+        both_add[0].wait_recv()
+        edge_ref[3] = mul(edge_ref[1] * one_decay, w_one) + one_add
+
+    own_map, own_add, own_decay = parts(prefix)
+    entering = mul(edge_ref[3] * own_decay, weights(own_map)) + own_add
 
     starts = [entering]
     for b in range(SUBS - 1):
@@ -239,6 +317,8 @@
         for b in range(SUBS):
             filt_ref[(b * length + i) * Q : (b * length + i + 1) * Q, :] = x[b * Q : (b + 1) * Q]
 
+    filt_copy = pltpu.make_async_copy(filt_ref, filt_out, out_sem.at[0])
+    filt_copy.start()
     next_copy.wait_recv()
     following = jnp.where(me == n - 1, 0.0, next_ref[:1, :])
     dx_ref[steps * Q : (steps + 1) * Q, :] = spread(following, Q)
@@ -246,6 +326,19 @@
     filtered = filt_ref[...]
     predicted = mul(filtered * ahead_decay, w_trans)
     g_ref[...] = filtered - mul(predicted * ahead_decay, w_gain)
+
+    z_total, suffix = take_back(count - 2, z_waiting, suffixes[-1])
+    suffixes.append(suffix)
+    back_ref[...] = z_total
+
+    @pl.when(top == 2)
+    def _():
+        for copy in back_two:
+            copy.start()
+
+    @pl.when(top == 1)
+    def _():
+        back_one.start()
 
     s = at(g_ref, length - 1)
     for i in range(length - 2, -1, -1):
@@ -262,9 +355,16 @@
         last = level == count - 1
         y_waiting = send(2, level, y_bufs, y)
         if last:
-            for copy in z_waiting:
-                copy.wait_recv()
-            w_later.append([weights(z_bufs[level][k]) for k in range(radix - 1)])
+
+            @pl.when(top <= 1)
+            def _():
+                back_two[0].wait_recv()
+
+            @pl.when(top == 0)
+            def _():
+                back_one.wait_recv()
+
+            w_later.append([None] + [weights(z_bufs[level][k]) for k in range(1, radix - 1)])
         for copy in y_waiting:
             copy.wait_recv()
         run = y_bufs[level][radix - 1]
@@ -290,9 +390,29 @@
             smooth_ref[(b * length + i) * Q : (b * length + i + 1) * Q, :] = s[b * Q : (b + 1) * Q]
         x = s * at(dx_ref, i)
 
+    smooth_copy = pltpu.make_async_copy(smooth_ref, smooth_out, out_sem.at[1])
+    smooth_copy.start()
+    @pl.when(top == 0)
+    def _():
+        first_add.wait_send()
+
+    @pl.when(top == 1)
+    def _():
+        back_one.wait_send()
+        for copy in both_add:
+            copy.wait_send()
+
+    @pl.when(top == 2)
+    def _():
+        third.wait_send()
+        for copy in back_two:
+            copy.wait_send()
+
     for copy in sent:
         copy.wait_send()
     next_copy.wait_send()
+    filt_copy.wait()
+    smooth_copy.wait()
 
 
 def levels_of(n):
@@ -312,13 +432,23 @@
         steps, records, channels = observations.shape
         rows = steps * records
         out = jax.ShapeDtypeStruct((rows, S), F32)
-        vmem = pl.BlockSpec(memory_space=pltpu.VMEM)
+        hbm = pl.BlockSpec(memory_space=pltpu.MemorySpace.HBM)
         filtered, smoothed = pl.pallas_call(
             functools.partial(kernel, n, levels),
             out_shape=(out, out),
-            in_specs=[vmem] * 6,
-            out_specs=(vmem, vmem),
+            in_specs=[hbm] * 6,
+            out_specs=(hbm, hbm),
             scratch_shapes=[
+                pltpu.VMEM((rows, channels), F32),
+                pltpu.VMEM(decay.shape, F32),
+                pltpu.VMEM((S, S), F32),
+                pltpu.VMEM(obs_map.shape, F32),
+                pltpu.VMEM((1, channels), F32),
+                pltpu.VMEM((S, S), F32),
+                pltpu.VMEM((rows, S), F32),
+                pltpu.VMEM((rows, S), F32),
+                pltpu.SemaphoreType.DMA((6,)),
+                pltpu.SemaphoreType.DMA((2,)),
                 pltpu.VMEM((rows, S), F32),
                 pltpu.VMEM((rows + 8, S), F32),
                 pltpu.VMEM((rows, S), F32),
@@ -326,12 +456,19 @@
                 pltpu.SemaphoreType.DMA,
                 pltpu.SemaphoreType.DMA,
             ]
-            + [pltpu.VMEM((radix, S + 16, S), F32) for radix, _ in levels]
+            + [pltpu.VMEM((radix, S + 16, S), F32) for radix, _ in levels[:-1]]
             + [pltpu.VMEM((radix, S, S), F32) for radix, _ in levels]
             + [pltpu.VMEM((radix, 8, S), F32) for radix, _ in levels]
-            + [pltpu.SemaphoreType.DMA((3, len(levels), 3))] * 2,
+            + [
+                pltpu.VMEM((S + 16, S), F32),
+                pltpu.VMEM((S + 16, S), F32),
+                pltpu.VMEM((S, S), F32),
+                pltpu.VMEM((4, 8, S), F32),
+            ]
+            + [pltpu.SemaphoreType.DMA((3, len(levels), 3))] * 2
+            + [pltpu.SemaphoreType.DMA((3,)), pltpu.SemaphoreType.DMA((5,))],
             compiler_params=pltpu.CompilerParams(
-                collective_id=0, has_side_effects=True, vmem_limit_bytes=48 * 2**20
+                collective_id=0, has_side_effects=True, vmem_limit_bytes=63 * 2**20
             ),
         )(
             observations.reshape(rows, channels),

time: 42.7 us -> 35.8 us (0.84)
  local copies, waits for them, and re-layouts: 5.9 us -> 2.14 us
  Pallas kernels: 35.7 us -> 32.8 us
    unnamed x14 -> x4, local copies, waits for them, and re-layouts: 5.9 us -> 2.14 us
    pallas_call x1, Pallas kernels: 35.7 us -> 32.8 us  [local(): pl.pallas_call(functools.partial(kernel, n, levels), out_shape=(out, out)...]
where the time goes in v1:
time: 35.8 us; the launch traced here: 35.6 us
  Pallas kernels  32.8 us (92%)
  local copies, waits for them, and re-layouts  2.14 us (6%)
  between operations  0.65 us (2%)
    pallas_call x1, Pallas kernels, local(): pl.pallas_call(functools.partial(kernel, n, levels), out_shape=(out, out)...  32.8 us
    unnamed x4, local copies, waits for them, and re-layouts  2.14 us

profile of v1, /device:TPU:0, one launch (start us, length us, event | category | flops | bytes accessed | tf_op | source)
XLA Modules:
  0.0 35.6 jit_solution(14857027647705023410)
XLA Ops:
  0.6 32.8 %shard_map.77 = (f32[128,128]{1,0:T(8,128)}, f32[128,128]{1,0:T(8,128)}) custom-call(f32[128,64]{1,0:T(8,128)} %bitcast.6, f32[32,128]{1,0:T(8,128)} %dec_in.1, f32[128,128]{1,0:T(8,128)} %trans_in.1, f32[64,128]{1,0:T(8,128)} %map_in.1, f32[1,64]{1,0:T(1,128)} %bitcast.7, f32[128,128]{1,0:T(8,128)} %gain_in.1), custom_call_target="tpu_custom_call" | custom-call | tf_op jit(solution)/shard_map/pallas_call | solution.py:436
  33.4 0.0 copy-start
  33.4 1.5 %copy.10 = f32[32,4,128]{2,1,0:T(4,128)} copy(f32[32,4,128]{2,1,0:T(4,128)} %bitcast.5) | data formatting | bytes 131072
  34.9 0.0 copy-done
  34.9 0.6 %copy.11 = f32[32,4,128]{2,1,0:T(4,128)} copy(f32[32,4,128]{2,1,0:T(4,128)S(1)} %bitcast.4) | data formatting | bytes 131072
Async XLA Ops:
  33.4 1.5 %copy-start = (f32[128,128]{1,0:T(8,128)S(1)}, f32[128,128]{1,0:T(8,128)}, u32[]{:S(2)}) copy-start(f32[128,128]{1,0:T(8,128)} %get-tuple-element.5) | copy-start | bytes 196612

commit v2 on v1

--- a/solution.py
+++ b/solution.py
@@ -87,7 +87,7 @@
     count = len(levels)
     f_bufs, rest = rest[: count - 1], rest[count - 1 :]
     z_bufs, y_bufs, rest = rest[:count], rest[count : 2 * count], rest[2 * count :]
-    own_ref, third_ref, back_ref, edge_ref, send_sem, recv_sem, edge_send, edge_recv = rest
+    own_ref, third_ref, edge_ref, send_sem, recv_sem, edge_send, edge_recv = rest
     fetched = [
         pltpu.make_async_copy(a, b, in_sem.at[k])
         for k, (a, b) in enumerate(
@@ -118,16 +118,25 @@
     pl.semaphore_signal(barrier, inc=1, device_id=((me + 1) % n,), device_id_type=MESH)
     greeted += 1
 
+    core = me % 2
+    sibling = me + 1 - 2 * core
+
+    def half(ref, slot):
+        rows = ref.shape[1] // 2
+        return ref.at[slot, pl.ds(pl.multiple_of(core * rows, 8), rows)]
+
     def send(which, level, bufs, own):
         radix, stride = levels[level]
-        digit = digits[level]
-        bufs[level][digit] = own
-        copies = []
+        digit, buf = digits[level], bufs[level]
+        buf[digit] = own
+        split = level > 0 and which < 2
+        source = half(buf, digit) if split else buf.at[digit]
+        copies, onward = [], []
         for ahead in range(1, radix):
             other = me + ((digit + ahead) % radix - digit) * stride
             copy = pltpu.make_async_remote_copy(
-                src_ref=bufs[level].at[digit],
-                dst_ref=bufs[level].at[digit],
+                src_ref=source,
+                dst_ref=source,
                 send_sem=send_sem.at[which, level, ahead - 1],
                 recv_sem=recv_sem.at[which, level, ahead - 1],
                 device_id=(other,),
@@ -135,8 +144,31 @@
             )
             copy.start()
             copies.append(copy)
-        sent.extend(copies)
-        return copies
+            if split:
+                arrived = half(buf, (digit - ahead) % radix)
+                onward.append(
+                    pltpu.make_async_remote_copy(
+                        src_ref=arrived,
+                        dst_ref=arrived,
+                        send_sem=send_sem.at[which, level, 2 + ahead],
+                        recv_sem=recv_sem.at[which, level, 2 + ahead],
+                        device_id=(sibling,),
+                        device_id_type=MESH,
+                    )
+                )
+        sent.extend(copies + onward)
+        return copies, onward
+
+    def relay(exchange):
+        copies, onward = exchange
+        for copy, more in zip(copies, onward):
+            copy.wait_recv()
+            more.start()
+
+    def collect(exchange):
+        copies, onward = exchange
+        for copy in onward or copies:
+            copy.wait_recv()
 
     sent = []
     for copy in fetched:
@@ -212,8 +244,7 @@
 
     def take_back(level, waiting, suffix):
         radix = levels[level][0]
-        for copy in waiting:
-            copy.wait_recv()
+        collect(waiting)
         z = [z_bufs[level][k] for k in range(radix)]
         w_z = [weights(z[k]) for k in range(radix - 1)]
         w_later.append(w_z)
@@ -239,15 +270,26 @@
     first_add = along(own_ref.at[pl.ds(S, 8)], edge_ref.at[0], 0, 0, 1)
     both_add = [along(edge_ref.at[2], edge_ref.at[1], k, 1, k) for k in (1, 2)]
     third = along(own_ref, third_ref, 0, 2, 1)
-    back_two = [along(back_ref, z_bufs[-1].at[2], k, 4, -k) for k in (1, 2)]
-    back_one = along(back_ref, z_bufs[-1].at[1], 1, 3, -1)
+    back_two = [along(half(z_bufs[-1], 2), half(z_bufs[-1], 2), k, 4, -k) for k in (1, 2)]
+    back_one = along(half(z_bufs[-1], 1), half(z_bufs[-1], 1), 1, 3, -1)
+    back_more = [
+        pltpu.make_async_remote_copy(
+            src_ref=half(z_bufs[-1], slot),
+            dst_ref=half(z_bufs[-1], slot),
+            send_sem=edge_send.at[2 + slot],
+            recv_sem=edge_recv.at[4 + slot],
+            device_id=(sibling,),
+            device_id_type=MESH,
+        )
+        for slot in (1, 2)
+    ]
 
     w_later, suffixes = [], [None]
     prefix = None
     for level in range(count - 1):
         radix = levels[level][0]
-        for copy in waiting:
-            copy.wait_recv()
+        relay(waiting)
+        collect(waiting)
         m = [f_bufs[level][k] for k in range(radix)]
         if radix == 2:
             options = [identity, m[0]]
@@ -275,6 +317,7 @@
         here = pick(digits[level], options)
         prefix = here if prefix is None else compose(here, prefix)
         if level < count - 2:
+            relay(z_waiting)
             z_total, suffix = take_back(level, z_waiting, suffixes[-1])
             suffixes.append(suffix)
 
@@ -307,6 +350,7 @@
     own_map, own_add, own_decay = parts(prefix)
     entering = mul(edge_ref[3] * own_decay, weights(own_map)) + own_add
 
+    relay(z_waiting)
     starts = [entering]
     for b in range(SUBS - 1):
         one_map, one_add, one_decay = parts(sub[b])
@@ -329,15 +373,16 @@
 
     z_total, suffix = take_back(count - 2, z_waiting, suffixes[-1])
     suffixes.append(suffix)
-    back_ref[...] = z_total
 
     @pl.when(top == 2)
     def _():
+        z_bufs[-1][2] = z_total
         for copy in back_two:
             copy.start()
 
     @pl.when(top == 1)
     def _():
+        z_bufs[-1][1] = z_total
         back_one.start()
 
     s = at(g_ref, length - 1)
@@ -354,19 +399,30 @@
     for level, (radix, stride) in enumerate(levels):
         last = level == count - 1
         y_waiting = send(2, level, y_bufs, y)
-        if last:
+        if level == count - 2:
 
             @pl.when(top <= 1)
             def _():
                 back_two[0].wait_recv()
+                back_more[1].start()
 
             @pl.when(top == 0)
             def _():
                 back_one.wait_recv()
+                back_more[0].start()
+
+        if last:
+
+            @pl.when(top <= 1)
+            def _():
+                back_more[1].wait_recv()
+
+            @pl.when(top == 0)
+            def _():
+                back_more[0].wait_recv()
 
             w_later.append([None] + [weights(z_bufs[level][k]) for k in range(1, radix - 1)])
-        for copy in y_waiting:
-            copy.wait_recv()
+        collect(y_waiting)
         run = y_bufs[level][radix - 1]
         options = [jnp.zeros((8, S), F32)]
         for k in range(radix - 2, -1, -1):
@@ -392,9 +448,14 @@
 
     smooth_copy = pltpu.make_async_copy(smooth_ref, smooth_out, out_sem.at[1])
     smooth_copy.start()
+    @pl.when(top <= 1)
+    def _():
+        back_more[1].wait_send()
+
     @pl.when(top == 0)
     def _():
         first_add.wait_send()
+        back_more[0].wait_send()
 
     @pl.when(top == 1)
     def _():
@@ -462,11 +523,10 @@
             + [
                 pltpu.VMEM((S + 16, S), F32),
                 pltpu.VMEM((S + 16, S), F32),
-                pltpu.VMEM((S, S), F32),
                 pltpu.VMEM((4, 8, S), F32),
             ]
-            + [pltpu.SemaphoreType.DMA((3, len(levels), 3))] * 2
-            + [pltpu.SemaphoreType.DMA((3,)), pltpu.SemaphoreType.DMA((5,))],
+            + [pltpu.SemaphoreType.DMA((3, len(levels), 6))] * 2
+            + [pltpu.SemaphoreType.DMA((5,)), pltpu.SemaphoreType.DMA((7,))],
             compiler_params=pltpu.CompilerParams(
                 collective_id=0, has_side_effects=True, vmem_limit_bytes=63 * 2**20
             ),

time: 35.8 us -> 35.9 us (level)
  no operation moved by 1% of the time
where the time goes in v2:
time: 35.9 us; the launch traced here: 35.7 us
  Pallas kernels  32.9 us (92%)
  local copies, waits for them, and re-layouts  2.14 us (6%)
  between operations  0.65 us (2%)
    pallas_call x1, Pallas kernels, local(): pl.pallas_call(functools.partial(kernel, n, levels), out_shape=(out, out)...  32.9 us
    unnamed x4, local copies, waits for them, and re-layouts  2.14 us

profile of v2, /device:TPU:0, one launch (start us, length us, event | category | flops | bytes accessed | tf_op | source)
XLA Modules:
  0.0 35.7 jit_solution(13758744544726723585)
XLA Ops:
  0.6 32.9 %shard_map.77 = (f32[128,128]{1,0:T(8,128)}, f32[128,128]{1,0:T(8,128)}) custom-call(f32[128,64]{1,0:T(8,128)} %bitcast.6, f32[32,128]{1,0:T(8,128)} %dec_in.1, f32[128,128]{1,0:T(8,128)} %trans_in.1, f32[64,128]{1,0:T(8,128)} %map_in.1, f32[1,64]{1,0:T(1,128)} %bitcast.7, f32[128,128]{1,0:T(8,128)} %gain_in.1), custom_call_target="tpu_custom_call" | custom-call | tf_op jit(solution)/shard_map/pallas_call | solution.py:497
  33.5 0.0 copy-start
  33.5 1.5 %copy.10 = f32[32,4,128]{2,1,0:T(4,128)} copy(f32[32,4,128]{2,1,0:T(4,128)} %bitcast.5) | data formatting | bytes 131072
  35.0 0.0 copy-done
  35.0 0.6 %copy.11 = f32[32,4,128]{2,1,0:T(4,128)} copy(f32[32,4,128]{2,1,0:T(4,128)S(1)} %bitcast.4) | data formatting | bytes 131072
Async XLA Ops:
  33.5 1.5 %copy-start = (f32[128,128]{1,0:T(8,128)S(1)}, f32[128,128]{1,0:T(8,128)}, u32[]{:S(2)}) copy-start(f32[128,128]{1,0:T(8,128)} %get-tuple-element.5) | copy-start | bytes 196612

commit v3 on v2

--- a/solution.py
+++ b/solution.py
@@ -288,6 +288,8 @@
     prefix = None
     for level in range(count - 1):
         radix = levels[level][0]
+        if level > 0:
+            z_waiting = send(1, level, z_bufs, z_total)
         relay(waiting)
         collect(waiting)
         m = [f_bufs[level][k] for k in range(radix)]
@@ -310,8 +312,6 @@
             def _():
                 third.start()
 
-        if level > 0:
-            z_waiting = send(1, level, z_bufs, z_total)
         if radix == 4:
             options = [identity, m[0], first, compose(first, m[2])]
         here = pick(digits[level], options)

time: 35.9 us -> 36.2 us (level)
  no operation moved by 1% of the time
where the time goes in v3:
time: 36.2 us; the launch traced here: 36 us
  Pallas kernels  33.2 us (92%)
  local copies, waits for them, and re-layouts  2.14 us (6%)
  between operations  0.65 us (2%)
    pallas_call x1, Pallas kernels, local(): pl.pallas_call(functools.partial(kernel, n, levels), out_shape=(out, out)...  33.2 us
    unnamed x4, local copies, waits for them, and re-layouts  2.14 us

profile of v3, /device:TPU:0, one launch (start us, length us, event | category | flops | bytes accessed | tf_op | source)
XLA Modules:
  0.0 36.0 jit_solution(1266219891544243900)
XLA Ops:
  0.6 33.2 %shard_map.77 = (f32[128,128]{1,0:T(8,128)}, f32[128,128]{1,0:T(8,128)}) custom-call(f32[128,64]{1,0:T(8,128)} %bitcast.6, f32[32,128]{1,0:T(8,128)} %dec_in.1, f32[128,128]{1,0:T(8,128)} %trans_in.1, f32[64,128]{1,0:T(8,128)} %map_in.1, f32[1,64]{1,0:T(1,128)} %bitcast.7, f32[128,128]{1,0:T(8,128)} %gain_in.1), custom_call_target="tpu_custom_call" | custom-call | tf_op jit(solution)/shard_map/pallas_call | solution.py:497
  33.9 0.0 copy-start
  33.9 1.5 %copy.10 = f32[32,4,128]{2,1,0:T(4,128)} copy(f32[32,4,128]{2,1,0:T(4,128)} %bitcast.5) | data formatting | bytes 131072
  35.4 0.0 copy-done
  35.4 0.6 %copy.11 = f32[32,4,128]{2,1,0:T(4,128)} copy(f32[32,4,128]{2,1,0:T(4,128)S(1)} %bitcast.4) | data formatting | bytes 131072
Async XLA Ops:
  33.9 1.5 %copy-start = (f32[128,128]{1,0:T(8,128)S(1)}, f32[128,128]{1,0:T(8,128)}, u32[]{:S(2)}) copy-start(f32[128,128]{1,0:T(8,128)} %get-tuple-element.5) | copy-start | bytes 196612

commit v4 on v1

--- a/solution.py
+++ b/solution.py
@@ -415,6 +415,17 @@
     smooth_copy.wait()
 
 
+def place(filt_in, smooth_in, filt_out, smooth_out, sem):
+    copies = [
+        pltpu.make_async_copy(filt_in, filt_out, sem.at[0]),
+        pltpu.make_async_copy(smooth_in, smooth_out, sem.at[1]),
+    ]
+    for copy in copies:
+        copy.start()
+    for copy in copies:
+        copy.wait()
+
+
 def levels_of(n):
     levels, stride = [], 1
     while stride < n:
@@ -478,6 +489,14 @@
             noise_precision.reshape(1, channels),
             smoother_gain,
         )
+        filtered, smoothed = pl.pallas_call(
+            place,
+            out_shape=(out, out),
+            in_specs=[hbm] * 2,
+            out_specs=(hbm, hbm),
+            scratch_shapes=[pltpu.SemaphoreType.DMA((2,))],
+            compiler_params=pltpu.CompilerParams(vmem_limit_bytes=63 * 2**20),
+        )(filtered, smoothed)
         return filtered.reshape(steps, records, S), smoothed.reshape(steps, records, S)
 
     in_specs = (P("tm", None, None), P("tm", None), P(), P(), P(), P())

time: 35.8 us -> 38.7 us (1.081)
  Pallas kernels: 32.8 us -> 37.9 us
  local copies, waits for them, and re-layouts: 2.14 us -> 0 us
    pallas_call x0 -> x1, Pallas kernels: none -> 5.09 us  [local(): pl.pallas_call(place, out_shape=(out, out), in_specs=[hbm] * 2, out_specs...]
    unnamed x4 -> x0, local copies, waits for them, and re-layouts: 2.14 us -> none
where the time goes in v4:
time: 38.7 us; the launch traced here: 38.5 us
  Pallas kernels  37.9 us (98%)
  between operations  0.64 us (2%)
    pallas_call x1, Pallas kernels, local(): pl.pallas_call(functools.partial(kernel, n, levels), out_shape=(out, out)...  32.8 us
    pallas_call x1, Pallas kernels, local(): pl.pallas_call(place, out_shape=(out, out), in_specs=[hbm] * 2, out_specs...  5.09 us

profile of v4, /device:TPU:0, one launch (start us, length us, event | category | flops | bytes accessed | tf_op | source)
XLA Modules:
  0.0 38.5 jit_solution(8954551873631975639)
XLA Ops:
  0.6 32.8 %shard_map.77 = (f32[128,128]{1,0:T(8,128)}, f32[128,128]{1,0:T(8,128)}) custom-call(f32[128,64]{1,0:T(8,128)} %bitcast.4, f32[32,128]{1,0:T(8,128)} %dec_in.1, f32[128,128]{1,0:T(8,128)} %trans_in.1, f32[64,128]{1,0:T(8,128)} %map_in.1, f32[1,64]{1,0:T(1,128)} %bitcast.5, f32[128,128]{1,0:T(8,128)} %gain_in.1), custom_call_target="tpu_custom_call" | custom-call | tf_op jit(solution)/shard_map/pallas_call | solution.py:447
  33.4 5.1 %shard_map.78 = (f32[128,128]{1,0:T(8,128)}, f32[128,128]{1,0:T(8,128)}) custom-call(f32[128,128]{1,0:T(8,128)} %get-tuple-element.6.filt_in, f32[128,128]{1,0:T(8,128)} %get-tuple-element.7.smooth_in), custom_call_target="tpu_custom_call" | custom-call | tf_op jit(solution)/shard_map/pallas_call | solution.py:492

commit v5 on v1

--- a/solution.py
+++ b/solution.py
@@ -327,19 +327,6 @@
     predicted = mul(filtered * ahead_decay, w_trans)
     g_ref[...] = filtered - mul(predicted * ahead_decay, w_gain)
 
-    z_total, suffix = take_back(count - 2, z_waiting, suffixes[-1])
-    suffixes.append(suffix)
-    back_ref[...] = z_total
-
-    @pl.when(top == 2)
-    def _():
-        for copy in back_two:
-            copy.start()
-
-    @pl.when(top == 1)
-    def _():
-        back_one.start()
-
     s = at(g_ref, length - 1)
     for i in range(length - 2, -1, -1):
         s = mul(s * at(dx_ref, i + 1), w_gain) + at(g_ref, i)
@@ -349,6 +336,19 @@
     y = r[SUBS - 1]
     for b in range(SUBS - 2, -1, -1):
         y = mul(y, w_sub[b]) + r[b]
+
+    z_total, suffix = take_back(count - 2, z_waiting, suffixes[-1])
+    suffixes.append(suffix)
+    back_ref[...] = z_total
+
+    @pl.when(top == 2)
+    def _():
+        for copy in back_two:
+            copy.start()
+
+    @pl.when(top == 1)
+    def _():
+        back_one.start()
 
     arriving = None
     for level, (radix, stride) in enumerate(levels):

time: 35.8 us -> 35.8 us (level)
  no operation moved by 1% of the time
where the time goes in v5:
time: 35.8 us; the launch traced here: 35.6 us
  Pallas kernels  32.8 us (92%)
  local copies, waits for them, and re-layouts  2.14 us (6%)
  between operations  0.65 us (2%)
    pallas_call x1, Pallas kernels, local(): pl.pallas_call(functools.partial(kernel, n, levels), out_shape=(out, out)...  32.8 us
    unnamed x4, local copies, waits for them, and re-layouts  2.14 us

profile of v5, /device:TPU:0, one launch (start us, length us, event | category | flops | bytes accessed | tf_op | source)
XLA Modules:
  0.0 35.6 jit_solution(10566445413243475197)
XLA Ops:
  0.6 32.8 %shard_map.77 = (f32[128,128]{1,0:T(8,128)}, f32[128,128]{1,0:T(8,128)}) custom-call(f32[128,64]{1,0:T(8,128)} %bitcast.6, f32[32,128]{1,0:T(8,128)} %dec_in.1, f32[128,128]{1,0:T(8,128)} %trans_in.1, f32[64,128]{1,0:T(8,128)} %map_in.1, f32[1,64]{1,0:T(1,128)} %bitcast.7, f32[128,128]{1,0:T(8,128)} %gain_in.1), custom_call_target="tpu_custom_call" | custom-call | tf_op jit(solution)/shard_map/pallas_call | solution.py:436
  33.4 0.0 copy-start
  33.4 1.5 %copy.10 = f32[32,4,128]{2,1,0:T(4,128)} copy(f32[32,4,128]{2,1,0:T(4,128)} %bitcast.5) | data formatting | bytes 131072
  34.9 0.0 copy-done
  34.9 0.6 %copy.11 = f32[32,4,128]{2,1,0:T(4,128)} copy(f32[32,4,128]{2,1,0:T(4,128)S(1)} %bitcast.4) | data formatting | bytes 131072
Async XLA Ops:
  33.4 1.5 %copy-start = (f32[128,128]{1,0:T(8,128)S(1)}, f32[128,128]{1,0:T(8,128)}, u32[]{:S(2)}) copy-start(f32[128,128]{1,0:T(8,128)} %get-tuple-element.5) | copy-start | bytes 196612
